TPU v7x, 32 devices: a whole 2x2x4 slice. The times are simulated.
32 devices in a mesh: groups: 2 (over x), frame: 16 (over z, y, core).
Axes of the slice: x: 2, y: 2, z: 4, core: 2. Of those that a mesh axis runs over, the one named last changes fastest.
Arguments:
- latent: bfloat16 [128, 32, 1152], P(('groups', 'frame')), parts along dimension 0, may hold values from -6 to 6
- ln_gain: float32 [1152], replicated, may hold values from 0.1 to 1.9
- q_gain: float32 [72], replicated, may hold values from 0.1 to 1.9
- k_gain: float32 [72], replicated, may hold values from 0.1 to 1.9
- w_qkv: bfloat16 [1152, 3456], replicated, may hold values from -0.1875 to 0.1875
- w_out: bfloat16 [1152, 1152], replicated, may hold values from -0.5 to 0.5
Outputs:
- result: bfloat16 [128, 32, 1152], P(('groups', 'frame')), parts along dimension 0
There are 2 independent parts, one for each index of `groups`. A program takes and returns all parts, laid end to end along the dimension named above; an argument that names none is the same for every part. Nothing has to cross between parts.
All inputs are finite; a program needn't handle non-finite values.
Results may differ from a plain program's by a relative error of at most 0.006.
Values may be sent and summed in bfloat16 or wider, within the bound.
No kernel may reach another device: no remote copies, remote signals or barrier semaphores. Data moves between devices by JAX's collectives and lax.ppermute only.
A program may use at most 64 MiB of HBM per device.

v0:
```python
import jax
import jax.numpy as jnp
from jax import lax
from jax.sharding import PartitionSpec as P

HEADS = 16
HEAD_DIM = 72


def layer_norm(rows, ln_gain):
    values = rows.astype(jnp.float32)
    center = values - jnp.mean(values, axis=-1, keepdims=True)
    spread = jnp.mean(center * center, axis=-1, keepdims=True)
    return (center * lax.rsqrt(spread + 1e-06) * ln_gain).astype(jnp.bfloat16)


def head_norm(values, gain):
    shaped = values.reshape(values.shape[:-1] + (HEADS, HEAD_DIM))
    mean_sq = jnp.mean(shaped * shaped, axis=-1, keepdims=True)
    return (shaped * lax.rsqrt(mean_sq + 1e-06) * gain).astype(jnp.bfloat16).reshape(values.shape)


def project(normed, w_qkv, q_gain, k_gain):
    width = normed.shape[-1]
    mixed = jnp.dot(normed.reshape(-1, width), w_qkv, preferred_element_type=jnp.float32)
    mixed = mixed.reshape(normed.shape[:-1] + (3 * width,))
    query = head_norm(mixed[..., :width], q_gain)
    keys = head_norm(mixed[..., width : 2 * width], k_gain)
    values = mixed[..., 2 * width :].astype(jnp.bfloat16)
    return (query, keys, values)


def attend(query, keys, values):
    lead = query.shape[0]
    others = query.shape[1]
    q_four = query.reshape(lead, others, HEADS, HEAD_DIM)
    k_four = keys.reshape(lead, others, HEADS, HEAD_DIM)
    v_four = values.reshape(lead, others, HEADS, HEAD_DIM)
    scores = jnp.einsum(
        "tshe,ushe->shtu", q_four, k_four, preferred_element_type=jnp.float32
    ) * HEAD_DIM ** (-0.5)
    weights = jnp.exp(scores)
    weights = (weights / jnp.sum(weights, axis=-1, keepdims=True)).astype(jnp.bfloat16)
    mixed = jnp.einsum("shtu,ushe->tshe", weights, v_four, preferred_element_type=jnp.float32)
    return mixed.astype(jnp.bfloat16).reshape(query.shape)


def body(latent, ln_gain, q_gain, k_gain, w_qkv, w_out):
    device_count = lax.axis_size("frame")
    rows, columns, model = latent.shape
    positions = rows * columns
    per_peer = positions // device_count
    flat = latent.reshape(positions, model)
    normed = layer_norm(flat, ln_gain)
    query, keys, values = project(
        lax.all_to_all(
            normed.reshape(device_count, per_peer, model),
            "frame",
            split_axis=0,
            concat_axis=0,
            tiled=True,
        ),
        w_qkv,
        q_gain,
        k_gain,
    )
    mixed = attend(query, keys, values)
    returned = lax.all_to_all(mixed, "frame", split_axis=0, concat_axis=0, tiled=True)
    attended = returned.reshape(positions, model)
    branch = jnp.dot(attended, w_out, preferred_element_type=jnp.float32)
    result = flat.astype(jnp.float32) + branch
    return result.astype(jnp.bfloat16).reshape(latent.shape)


def solution(mesh):
    placed = (P(("groups", "frame"), None, None), P(), P(), P(), P(), P())
    return jax.shard_map(
        body,
        mesh=mesh,
        in_specs=placed,
        out_specs=P(("groups", "frame"), None, None),
        check_vma=False,
    )
```

profile of v0, /device:TPU:0, one launch (start us, length us, event | category | flops | bytes accessed | tf_op | source)
XLA Modules:
  0.0 64.0 jit_solution(6574092277274631922)
XLA Ops:
  0.0 0.0 copy-start
  0.0 1.2 %convert_reduce_fusion = f32[4,32]{1,0:T(4,128)S(1)} fusion(bf16[4,32,1152]{2,1,0:T(8,128)(2,1)} %param.6), kind=kLoop, calls=%fused_computation.21 | loop fusion | flops 294784 | bytes 295424 | tf_op jit(solution)/shard_map/reduce_sum | solution.py:12
  1.2 1.2 %multiply_reduce_fusion.2 = f32[4,32]{1,0:T(4,128)S(1)} fusion(bf16[4,32,1152]{2,1,0:T(8,128)(2,1)} %param.6, f32[4,32]{1,0:T(4,128)S(1)} %broadcast_multiply_fusion), kind=kLoop, calls=%fused_computation.15 | loop fusion | flops 589696 | bytes 295936 | tf_op jit(solution)/shard_map/reduce_sum | solution.py:13
  2.4 0.1 div.23
  2.5 1.0 %convert_element_type.52 = f32[4,32,1152]{2,1,0:T(8,128)S(1)} convert(bf16[4,32,1152]{2,1,0:T(8,128)(2,1)} %param.6) | non-fusion elementwise | flops 147456 | bytes 884736 | tf_op jit(solution)/shard_map/convert_element_type | solution.py:71
  3.5 0.1 rsqrt.28
  3.6 0.8 %multiply_convert_fusion.2 = bf16[16,8,1152]{2,1,0:T(8,128)(2,1)S(1)} fusion(f32[16,8,1152]{2,1,0:T(8,128)S(1)} %bitcast.16, f32[1152]{0:T(1024)} %param.7, f32[16,8]{1,0:T(8,128)S(1)} %rsqrt.28, f32[16,8]{1,0:T(8,128)S(1)} %div.23), kind=kLoop, calls=%fused_computation.14 | loop fusion | flops 589824 | bytes 890368 | tf_op jit(solution)/shard_map/convert_element_type | solution.py:14
  4.5 17.8 %all_to_all.10 = bf16[16,8,1152]{2,1,0:T(8,128)(2,1)S(1)} all-to-all(bf16[16,8,1152]{2,1,0:T(8,128)(2,1)S(1)} %multiply_convert_fusion.2), channel_id=1, replica_groups=mesh['groups'=2,'frame'=16] {'frame'}, dimensions={0} | all-to-all | bytes 589824 | tf_op jit(solution)/shard_map/all_to_all | solution.py:56
  22.2 4.6 %fusion = f32[16,8,3456]{2,1,0:T(8,128)S(1)} fusion(bf16[16,8,1152]{2,1,0:T(8,128)(2,1)S(1)} %all_to_all.10, bf16[1152,3456]{1,0:T(8,128)(2,1)} %param.10), kind=kOutput, calls=%fused_computation | convolution fusion | flops 1019215872 | bytes 10027008 | tf_op jit(solution)/shard_map/dot_general | solution.py:25
  26.9 1.1 %fusion.18 = (f32[16,8,1152]{2,1,0:T(8,128)}, f32[16,8,1152]{2,1,0:T(8,128)}) fusion(f32[16,8,3456]{2,1,0:T(8,128)S(1)} %fusion), kind=kLoop, calls=%fused_computation.29 | loop fusion | bytes 2359296 | tf_op jit(solution)/shard_map/slice | solution.py:27
  28.0 1.8 %reshape.96 = bf16[16,8,16,72]{3,2,1,0:T(8,128)(2,1)} reshape(bf16[16,8,1152]{2,1,0:T(8,128)(2,1)S(1)} %slice.17) | data formatting | bytes 589824 | tf_op jit(solution)/shard_map/reshape | solution.py:38
  29.7 0.0 copy-start.1
  29.7 0.0 copy-start.2
  29.7 2.9 %reshape.97 = f32[16,8,16,72]{3,2,1,0:T(8,128)} reshape(f32[16,8,1152]{2,1,0:T(8,128)} %get-tuple-element.5) | data formatting | bytes 1179648 | tf_op jit(solution)/shard_map/reshape | solution.py:18
  32.7 1.6 %multiply_reduce_fusion.1 = f32[16,8,16]{2,1,0:T(8,128)S(1)} fusion(f32[16,8,16,72]{3,2,1,0:T(8,128)} %reshape.97), kind=kLoop, calls=%fused_computation.12 | loop fusion | flops 292864 | bytes 598016 | tf_op jit(solution)/shard_map/reduce_sum | solution.py:19
  34.3 3.0 %reshape.98 = f32[16,8,16,72]{3,2,1,0:T(8,128)} reshape(f32[16,8,1152]{2,1,0:T(8,128)} %get-tuple-element.6) | data formatting | bytes 1179648 | tf_op jit(solution)/shard_map/reshape | solution.py:18
  37.3 1.6 %multiply_reduce_fusion = f32[16,8,16]{2,1,0:T(8,128)S(1)} fusion(f32[16,8,16,72]{3,2,1,0:T(8,128)} %reshape.98), kind=kLoop, calls=%fused_computation.10 | loop fusion | flops 292864 | bytes 598016 | tf_op jit(solution)/shard_map/reduce_sum | solution.py:19
  38.9 0.0 copy-done.1
  38.9 0.0 copy-done.2
  38.9 1.9 %multiply_convert_fusion = (bf16[16,8,16,72]{3,2,1,0:T(8,128)(2,1)S(1)}, bf16[16,8,16,72]{3,2,1,0:T(8,128)(2,1)S(1)}) fusion(f32[16,8,16,72]{3,2,1,0:T(8,128)} %reshape.98, f32[72]{0:T(128)S(1)} %copy-done.1, f32[16,8,16]{2,1,0:T(8,128)S(1)} %add_rsqrt_fusion, f32[72]{0:T(128)S(1)} %copy-done.2, f32[16,8,16,72]{3,2,1,0:T(8,128)} %reshape.97, ...), kind=kLoop, calls=%fused_computation.9 | loop fusion | flops 884736 | bytes 1786432 | tf_op jit(solution)/shard_map/convert_element_type | solution.py:20
  40.8 1.8 %fusion.3 = f32[8,16,16,16]{2,3,1,0:T(8,128)} fusion(bf16[16,8,16,72]{3,2,1,0:T(8,128)(2,1)S(1)} %get-tuple-element.7, bf16[16,8,16,72]{3,2,1,0:T(8,128)(2,1)S(1)} %get-tuple-element.8), kind=kOutput, calls=%fused_computation.5 | convolution fusion | flops 4751360 | bytes 720896 | tf_op jit(solution)/shard_map/tshe,ushe->shtu/dot_general | solution.py:39
  42.6 3.1 %fusion.4 = bf16[16,8,16,72]{3,0,2,1:T(8,128)(2,1)} fusion(f32[8,16,16,16]{2,3,1,0:T(8,128)} %fusion.3, bf16[16,8,16,72]{3,2,1,0:T(8,128)(2,1)} %reshape.96), kind=kOutput, calls=%fused_computation.7 | convolution fusion | flops 4933647 | bytes 720896 | tf_op jit(solution)/shard_map/shtu,ushe->tshe/dot_general | solution.py:44
  45.7 2.0 %copy.20 = bf16[16,8,16,72]{3,2,1,0:T(8,128)(2,1)} copy(bf16[16,8,16,72]{3,0,2,1:T(8,128)(2,1)} %fusion.4) | data formatting | bytes 589824 | tf_op jit(solution)/shard_map/convert_element_type | solution.py:45
  47.7 1.5 %reshape.99 = bf16[16,8,1152]{2,1,0:T(8,128)(2,1)S(1)} reshape(bf16[16,8,16,72]{3,2,1,0:T(8,128)(2,1)} %copy.20) | data formatting | bytes 589824 | tf_op jit(solution)/shard_map/reshape | solution.py:45
  49.2 13.5 %all_to_all.11 = bf16[16,8,1152]{2,1,0:T(8,128)(2,1)S(1)} all-to-all(bf16[16,8,1152]{2,1,0:T(8,128)(2,1)S(1)} %reshape.99), channel_id=1, replica_groups=mesh['groups'=2,'frame'=16] {'frame'}, dimensions={0} | all-to-all | bytes 589824 | tf_op jit(solution)/shard_map/all_to_all | solution.py:68
  62.7 0.0 copy-done
  62.7 1.3 %fusion.2 = bf16[128,1152]{1,0:T(8,128)(2,1)} fusion(f32[128,1152]{1,0:T(8,128)S(1)} %bitcast.17, bf16[1152,1152]{1,0:T(8,128)(2,1)S(1)} %copy-done, bf16[16,8,1152]{2,1,0:T(8,128)(2,1)S(1)} %all_to_all.11), kind=kOutput, calls=%fused_computation.3 | convolution fusion | flops 340033536 | bytes 3833856 | tf_op jit(solution)/shard_map/dot_general | solution.py:70
  (5 shorter events, 0.1 us)
Async XLA Ops:
  0.0 62.7 %copy-start = (bf16[1152,1152]{1,0:T(8,128)(2,1)S(1)}, bf16[1152,1152]{1,0:T(8,128)(2,1)}, u32[]{:S(2)}) copy-start(bf16[1152,1152]{1,0:T(8,128)(2,1)} %param.11) | copy-start | bytes 7962628
  29.7 9.1 %copy-start.1 = (f32[72]{0:T(128)S(1)}, f32[72]{0:T(128)}, u32[]{:S(2)}) copy-start(f32[72]{0:T(128)} %param.9) | copy-start | bytes 868
  29.7 9.1 %copy-start.2 = (f32[72]{0:T(128)S(1)}, f32[72]{0:T(128)}, u32[]{:S(2)}) copy-start(f32[72]{0:T(128)} %param.8) | copy-start | bytes 868
where the time goes:
time: 64.6 us; the launch traced here: 64 us
  blocking collectives  31.2 us (48%)
  local copies, waits for them, and re-layouts  12.5 us (19%)
  matrix products  10.8 us (17%)
  other arithmetic  9.38 us (15%)
    all_to_all x1, blocking collectives, body(): lax.all_to_all(normed.reshape(device_count, per_peer, model), 'frame', sp...  17.8 us
    all_to_all x1, blocking collectives, body(): lax.all_to_all(mixed, 'frame', split_axis=0, concat_axis=0, tiled=True)  13.5 us
    reshape x2, local copies, waits for them, and re-layouts, head_norm(): shaped = values.reshape(values.shape[:-1] + (HEADS, HEAD_DIM))  5.91 us
    dot_general x1, matrix products, project(): jnp.dot(normed.reshape(-1, width), w_qkv, preferred_element_type=jnp.floa...  4.61 us
    reduce_sum x2, other arithmetic, head_norm(): mean_sq = jnp.mean(shaped * shaped, axis=-1, keepdims=True)  3.14 us
    dot_general x1, matrix products, attend(): jnp.einsum('shtu,ushe->tshe', weights, v_four, preferred_element_type=jnp...  3.11 us
    convert_element_type x1, local copies, waits for them, and re-layouts, attend(): return mixed.astype(jnp.bfloat16).reshape(query.shape)  1.97 us
    convert_element_type x1, other arithmetic, head_norm(): (shaped * lax.rsqrt(mean_sq + 1e-06) * gain).astype(jnp.bfloat16)  1.92 us

commit v1 on v0

v1 whole, which is shorter than its diff:
```python
import functools

import jax
import jax.numpy as jnp
from jax import lax
from jax.experimental import pallas as pl
from jax.experimental.pallas import tpu as pltpu
from jax.sharding import PartitionSpec as P

HEADS = 16
HEAD_DIM = 72
LANES = 128
EPS = 1e-06


def tokens_kernel(
    positions, x_ref, ln_ref, qg_ref, kg_ref, wqkv_ref, wout_ref, o_ref, normed, queries, keys, values, attended
):
    tokens, width = x_ref.shape
    bf16 = jnp.bfloat16

    gain = ln_ref[...]
    for row in range(0, tokens, 16):
        rows = pl.ds(row, 16)
        x = x_ref[rows, :].astype(jnp.float32)
        center = x - jnp.mean(x, axis=-1, keepdims=True)
        spread = jnp.mean(center * center, axis=-1, keepdims=True)
        normed[rows, :] = (center * lax.rsqrt(spread + EPS) * gain).astype(bf16)

    feature = lax.broadcasted_iota(jnp.int32, (width, LANES), 0)
    first = lax.broadcasted_iota(jnp.int32, (width, LANES), 1) * HEAD_DIM
    member = ((feature >= first) & (feature < first + HEAD_DIM)).astype(bf16)
    feature = lax.broadcasted_iota(jnp.int32, (LANES, width), 1)
    first = lax.broadcasted_iota(jnp.int32, (LANES, width), 0) * HEAD_DIM
    spread_out = ((feature >= first) & (feature < first + HEAD_DIM)).astype(bf16)

    def dot(a, b):
        return jnp.dot(a, b, preferred_element_type=jnp.float32)

    def head_norm(part, head_gain, out):
        mixed = dot(normed[...], wqkv_ref[:, part * width : (part + 1) * width])
        squares = mixed * mixed
        high = squares.astype(bf16)
        low = (squares - high.astype(jnp.float32)).astype(bf16)
        total = dot(high, member) + dot(low, member)
        inverse = lax.rsqrt(total * (1.0 / HEAD_DIM) + EPS)
        high = inverse.astype(bf16)
        low = (inverse - high.astype(jnp.float32)).astype(bf16)
        scale = dot(high, spread_out) + dot(low, spread_out)
        full_gain = jnp.concatenate([head_gain] * HEADS, axis=1)
        out[...] = (mixed * scale * full_gain).astype(bf16)

    head_norm(0, qg_ref[...], queries)
    head_norm(1, kg_ref[...], keys)
    values[...] = dot(normed[...], wqkv_ref[:, 2 * width :]).astype(bf16)

    place = lax.broadcasted_iota(jnp.int32, (tokens, tokens), 0) % positions
    other = lax.broadcasted_iota(jnp.int32, (tokens, tokens), 1) % positions
    same = place == other
    held = {}
    for head in range(HEADS):
        begin, end = head * HEAD_DIM, (head + 1) * HEAD_DIM
        low, high = begin // LANES, -(-end // LANES)
        window = slice(low * LANES, high * LANES)
        lane = lax.broadcasted_iota(jnp.int32, (1, (high - low) * LANES), 1) + low * LANES
        mine = (lane >= begin) & (lane < end)
        query = jnp.where(mine, queries[:, window], jnp.zeros((), bf16))
        scores = lax.dot_general(
            query, keys[:, window], (((1,), (1,)), ((), ())), preferred_element_type=jnp.float32
        ) * HEAD_DIM ** (-0.5)
        weights = jnp.where(same, jnp.exp(scores), 0.0)
        weights = (weights / jnp.sum(weights, axis=-1, keepdims=True)).astype(bf16)
        value = jnp.where(mine, values[:, window], jnp.zeros((), bf16))
        mixed = dot(weights, value)
        for tile in range(low, high):
            piece = mixed[:, (tile - low) * LANES : (tile - low + 1) * LANES]
            held[tile] = held[tile] + piece if tile in held else piece
            if end >= (tile + 1) * LANES:
                attended[:, tile * LANES : (tile + 1) * LANES] = held.pop(tile).astype(bf16)

    branch = dot(attended[...], wout_ref[...])
    o_ref[...] = (x_ref[...].astype(jnp.float32) + branch).astype(bf16)


def body(latent, ln_gain, q_gain, k_gain, w_qkv, w_out):
    device_count = lax.axis_size("frame")
    rows, columns, model = latent.shape
    tokens = rows * columns
    per_peer = tokens // device_count
    exchange = functools.partial(
        lax.all_to_all, axis_name="frame", split_axis=0, concat_axis=0, tiled=True
    )
    gathered = exchange(latent.reshape(device_count, per_peer, model))
    block = functools.partial(pltpu.VMEM, dtype=jnp.bfloat16)
    result = pl.pallas_call(
        functools.partial(tokens_kernel, per_peer),
        out_shape=jax.ShapeDtypeStruct((tokens, model), jnp.bfloat16),
        in_specs=[pl.BlockSpec(memory_space=pltpu.VMEM)] * 6,
        out_specs=pl.BlockSpec(memory_space=pltpu.VMEM),
        scratch_shapes=[block((tokens, model)) for _ in range(5)],
        compiler_params=pltpu.CompilerParams(vmem_limit_bytes=32 * 1024 * 1024),
        name="tokens",
    )(
        gathered.reshape(tokens, model),
        ln_gain.reshape(1, model),
        q_gain.reshape(1, HEAD_DIM),
        k_gain.reshape(1, HEAD_DIM),
        w_qkv,
        w_out,
    )
    return exchange(result.reshape(device_count, per_peer, model)).reshape(latent.shape)


def solution(mesh):
    placed = (P(("groups", "frame"), None, None), P(), P(), P(), P(), P())
    return jax.shard_map(
        body,
        mesh=mesh,
        in_specs=placed,
        out_specs=P(("groups", "frame"), None, None),
        check_vma=False,
    )
```

time: 64.6 us -> 44.4 us (0.69)
  blocking collectives: 31.2 us -> 13.5 us
  matrix products: 10.8 us -> 0 us
  waiting for transfers between devices: 0 us -> 9.87 us
  other arithmetic: 9.38 us -> 0 us
  starting transfers between devices: 0 us -> 7.39 us
  Pallas kernels: 0 us -> 5.51 us
  local copies, waits for them, and re-layouts: 12.5 us -> 7.74 us
    all_to_all x2 -> x1, blocking collectives: 31.2 us -> 13.5 us  [body(): exchange(result.reshape(device_count, per_peer, model))]
    dot_general x4 -> x0, matrix products: 10.8 us -> none  [the longest x1 4.61 us: project(): jnp.dot(normed.reshape(-1, width), w_qkv, preferred_element_type=jnp.floa...]
    all_to_all x0 -> x1, waiting for transfers between devices: none -> 9.87 us  [body(): gathered = exchange(latent.reshape(device_count, per_peer, model))]
    reshape x4 -> x1, local copies, waits for them, and re-layouts: 9.22 us -> 0.7 us  [body(): ln_gain.reshape(1, model)]
    all_to_all x0 -> x1, starting transfers between devices: none -> 7.39 us  [body(): gathered = exchange(latent.reshape(device_count, per_peer, model))]
    unnamed x6 -> x9, local copies, waits for them, and re-layouts: 0.01 us -> 7.03 us
    reduce_sum x4 -> x0, other arithmetic: 5.55 us -> none  [the longest x2 3.14 us: head_norm(): mean_sq = jnp.mean(shaped * shaped, axis=-1, keepdims=True)]
    pallas_call x0 -> x1, Pallas kernels: none -> 5.51 us  [body(): pl.pallas_call(functools.partial(tokens_kernel, per_peer), out_shape=jax....]
  transfers between devices with their start and end apart: 0 -> 1, of which waited for: 0 -> 1; matrix products, arithmetic and copies ran while one was open for 0% -> 2% of each run, Pallas kernels for 0% -> 0%
where the time goes in v1:
time: 44.4 us; the launch traced here: 44 us
  blocking collectives  13.5 us (30%)
  waiting for transfers between devices  9.87 us (22%)
  local copies, waits for them, and re-layouts  7.74 us (17%)
  starting transfers between devices  7.39 us (17%)
  Pallas kernels  5.51 us (12%)
    all_to_all x1, blocking collectives, body(): exchange(result.reshape(device_count, per_peer, model))  13.5 us
    all_to_all x1, waiting for transfers between devices, body(): gathered = exchange(latent.reshape(device_count, per_peer, model))  9.87 us
    all_to_all x1, starting transfers between devices, body(): gathered = exchange(latent.reshape(device_count, per_peer, model))  7.39 us
    unnamed x9, local copies, waits for them, and re-layouts  7.03 us
    pallas_call x1, Pallas kernels, body(): pl.pallas_call(functools.partial(tokens_kernel, per_peer), out_shape=jax....  5.51 us
  transfers between devices with their start and end apart: 1, of which 1 were waited for; matrix products, arithmetic and copies ran while one was open for 2% of the time, Pallas kernels for 0%

profile of v1, /device:TPU:0, one launch (start us, length us, event | category | flops | bytes accessed | tf_op | source)
XLA Modules:
  0.0 44.0 jit_solution(11988729073447330740)
XLA Ops:
  0.0 7.4 %all-to-all-start = ((bf16[16,8,1152]{2,1,0:T(8,128)(2,1)}), bf16[16,8,1152]{2,1,0:T(8,128)(2,1)S(1)}, u32[]{:S(2)}, u32[]{:S(2)}) async-start(bf16[16,8,1152]{2,1,0:T(8,128)(2,1)} %bitcast.11), calls=%async_computation | async-start | bytes 589824 | tf_op jit(solution)/shard_map/all_to_all | solution.py:93
  7.4 0.7 %reshape.23.ln_ref = f32[1,1152]{1,0:T(1,128)S(1)} reshape(f32[1152]{0:T(1024)} %param.7) | data formatting | bytes 9216 | tf_op jit(solution)/shard_map/reshape | solution.py:105
  8.1 9.9 %all-to-all-done = bf16[16,8,1152]{2,1,0:T(8,128)(2,1)S(1)} async-done(((bf16[16,8,1152]{2,1,0:T(8,128)(2,1)}), bf16[16,8,1152]{2,1,0:T(8,128)(2,1)S(1)}, u32[]{:S(2)}, u32[]{:S(2)}) %all-to-all-start) | async-done | bytes 294944 | tf_op jit(solution)/shard_map/all_to_all | solution.py:93
  18.0 0.0 copy-start
  18.0 3.3 %copy-done = bf16[1152,3456]{1,0:T(8,128)(2,1)S(1)} copy-done((bf16[1152,3456]{1,0:T(8,128)(2,1)S(1)}, bf16[1152,3456]{1,0:T(8,128)(2,1)}, u32[]{:S(2)}) %copy-start) | copy-done | bytes 7962648
  21.2 0.0 copy-start.1
  21.2 1.7 %copy-done.1 = bf16[1152,1152]{1,0:T(8,128)(2,1)S(1)} copy-done((bf16[1152,1152]{1,0:T(8,128)(2,1)S(1)}, bf16[1152,1152]{1,0:T(8,128)(2,1)}, u32[]{:S(2)}) %copy-start.1) | copy-done | bytes 2654232
  23.0 0.0 copy-start.2
  23.0 0.7 %copy-done.2 = f32[72]{0:T(128)S(1)} copy-done((f32[72]{0:T(128)S(1)}, f32[72]{0:T(128)}, u32[]{:S(2)}) %copy-start.2) | copy-done | bytes 312
  23.6 0.0 copy-start.3
  23.6 0.7 %copy-done.3 = f32[72]{0:T(128)S(1)} copy-done((f32[72]{0:T(128)S(1)}, f32[72]{0:T(128)}, u32[]{:S(2)}) %copy-start.3) | copy-done | bytes 312
  24.3 5.5 %tokens.1 = bf16[128,1152]{1,0:T(8,128)(2,1)S(1)} custom-call(bf16[128,1152]{1,0:T(8,128)(2,1)S(1)} %bitcast.6, f32[1,1152]{1,0:T(1,128)S(1)} %reshape.23.ln_ref, f32[1,72]{1,0:T(1,128)S(1)} %bitcast.8, f32[1,72]{1,0:T(1,128)S(1)} %bitcast.9, bf16[1152,3456]{1,0:T(8,128)(2,1)S(1)} %copy-done, bf16[1152,1152]{1,0:T(8,128)(2,1)S(1)} %copy-done.1), custom_call_target="tpu_custom_call" | custom-call | tf_op jit(solution)/shard_map/tokens/pallas_call | solution.py:95
  29.8 13.5 %all_to_all.10 = bf16[16,8,1152]{2,1,0:T(8,128)(2,1)S(1)} all-to-all(bf16[16,8,1152]{2,1,0:T(8,128)(2,1)S(1)} %bitcast.7), channel_id=1, replica_groups=mesh['groups'=2,'frame'=16] {'frame'}, dimensions={0} | all-to-all | bytes 589824 | tf_op jit(solution)/shard_map/all_to_all | solution.py:111
  43.3 0.7 %copy.8 = bf16[4,32,1152]{2,1,0:T(8,128)(2,1)} copy(bf16[4,32,1152]{2,1,0:T(8,128)(2,1)S(1)} %bitcast.10) | data formatting | bytes 589824
Async XLA Ops:
  0.0 18.0 %all-to-all-start = ((bf16[16,8,1152]{2,1,0:T(8,128)(2,1)}), bf16[16,8,1152]{2,1,0:T(8,128)(2,1)S(1)}, u32[]{:S(2)}, u32[]{:S(2)}) async-start(bf16[16,8,1152]{2,1,0:T(8,128)(2,1)} %bitcast.11), calls=%async_computation | async-start | bytes 589824 | tf_op jit(solution)/shard_map/all_to_all | solution.py:93
  18.0 3.3 %copy-start = (bf16[1152,3456]{1,0:T(8,128)(2,1)S(1)}, bf16[1152,3456]{1,0:T(8,128)(2,1)}, u32[]{:S(2)}) copy-start(bf16[1152,3456]{1,0:T(8,128)(2,1)} %wqkv_ref.1) | copy-start | bytes 23887876
  21.2 1.7 %copy-start.1 = (bf16[1152,1152]{1,0:T(8,128)(2,1)S(1)}, bf16[1152,1152]{1,0:T(8,128)(2,1)}, u32[]{:S(2)}) copy-start(bf16[1152,1152]{1,0:T(8,128)(2,1)} %wout_ref.1) | copy-start | bytes 7962628
  23.0 0.7 %copy-start.2 = (f32[72]{0:T(128)S(1)}, f32[72]{0:T(128)}, u32[]{:S(2)}) copy-start(f32[72]{0:T(128)} %param.8) | copy-start | bytes 868
  23.6 0.7 %copy-start.3 = (f32[72]{0:T(128)S(1)}, f32[72]{0:T(128)}, u32[]{:S(2)}) copy-start(f32[72]{0:T(128)} %param.9) | copy-start | bytes 868

commit v2 on v1

--- a/solution.py
+++ b/solution.py
@@ -13,13 +13,35 @@
 EPS = 1e-06
 
 
+def weights_kernel(
+    ln_ref, qg_ref, kg_ref, wqkv_ref, wout_ref, gains_out, wqkv_out, wout_out, ln_held, qg_held, kg_held, sems
+):
+    pairs = [
+        (wqkv_ref, wqkv_out),
+        (wout_ref, wout_out),
+        (ln_ref, ln_held),
+        (qg_ref, qg_held),
+        (kg_ref, kg_held),
+    ]
+    copies = [pltpu.make_async_copy(src, dst, sems.at[i]) for i, (src, dst) in enumerate(pairs)]
+    for copy in copies:
+        copy.start()
+    for copy in copies[2:]:
+        copy.wait()
+    gains_out[0:1, :] = ln_held[...].reshape(1, -1)
+    gains_out[1:2, :] = jnp.concatenate([qg_held[...].reshape(1, -1)] * HEADS, axis=1)
+    gains_out[2:3, :] = jnp.concatenate([kg_held[...].reshape(1, -1)] * HEADS, axis=1)
+    for copy in copies[:2]:
+        copy.wait()
+
+
 def tokens_kernel(
-    positions, x_ref, ln_ref, qg_ref, kg_ref, wqkv_ref, wout_ref, o_ref, normed, queries, keys, values, attended
+    positions, x_ref, gains_ref, wqkv_ref, wout_ref, o_ref, normed, queries, keys, values, attended
 ):
     tokens, width = x_ref.shape
     bf16 = jnp.bfloat16
 
-    gain = ln_ref[...]
+    gain = gains_ref[0:1, :]
     for row in range(0, tokens, 16):
         rows = pl.ds(row, 16)
         x = x_ref[rows, :].astype(jnp.float32)
@@ -37,7 +59,7 @@
     def dot(a, b):
         return jnp.dot(a, b, preferred_element_type=jnp.float32)
 
-    def head_norm(part, head_gain, out):
+    def head_norm(part, out):
         mixed = dot(normed[...], wqkv_ref[:, part * width : (part + 1) * width])
         squares = mixed * mixed
         high = squares.astype(bf16)
@@ -47,11 +69,10 @@
         high = inverse.astype(bf16)
         low = (inverse - high.astype(jnp.float32)).astype(bf16)
         scale = dot(high, spread_out) + dot(low, spread_out)
-        full_gain = jnp.concatenate([head_gain] * HEADS, axis=1)
-        out[...] = (mixed * scale * full_gain).astype(bf16)
+        out[...] = (mixed * scale * gains_ref[part + 1 : part + 2, :]).astype(bf16)
 
-    head_norm(0, qg_ref[...], queries)
-    head_norm(1, kg_ref[...], keys)
+    head_norm(0, queries)
+    head_norm(1, keys)
     values[...] = dot(normed[...], wqkv_ref[:, 2 * width :]).astype(bf16)
 
     place = lax.broadcasted_iota(jnp.int32, (tokens, tokens), 0) % positions
@@ -90,24 +111,40 @@
     exchange = functools.partial(
         lax.all_to_all, axis_name="frame", split_axis=0, concat_axis=0, tiled=True
     )
+    in_vmem = pl.BlockSpec(memory_space=pltpu.VMEM)
+    in_hbm = pl.BlockSpec(memory_space=pltpu.HBM)
+    gains, wqkv_held, wout_held = pl.pallas_call(
+        weights_kernel,
+        out_shape=(
+            pltpu.VMEM((8, model), jnp.float32),
+            pltpu.VMEM(w_qkv.shape, w_qkv.dtype),
+            pltpu.VMEM(w_out.shape, w_out.dtype),
+        ),
+        in_specs=[in_hbm] * 5,
+        out_specs=[in_vmem] * 3,
+        scratch_shapes=[
+            pltpu.VMEM((model,), jnp.float32),
+            pltpu.VMEM((HEAD_DIM,), jnp.float32),
+            pltpu.VMEM((HEAD_DIM,), jnp.float32),
+            pltpu.SemaphoreType.DMA((5,)),
+        ],
+        compiler_params=pltpu.CompilerParams(vmem_limit_bytes=16 * 1024 * 1024),
+        cost_estimate=pl.CostEstimate(
+            flops=0, bytes_accessed=2 * (w_qkv.size + w_out.size) * 2, transcendentals=0
+        ),
+        name="weights",
+    )(*(pltpu.with_memory_space_constraint(a, pltpu.HBM) for a in (ln_gain, q_gain, k_gain, w_qkv, w_out)))
     gathered = exchange(latent.reshape(device_count, per_peer, model))
     block = functools.partial(pltpu.VMEM, dtype=jnp.bfloat16)
     result = pl.pallas_call(
         functools.partial(tokens_kernel, per_peer),
         out_shape=jax.ShapeDtypeStruct((tokens, model), jnp.bfloat16),
-        in_specs=[pl.BlockSpec(memory_space=pltpu.VMEM)] * 6,
-        out_specs=pl.BlockSpec(memory_space=pltpu.VMEM),
+        in_specs=[in_vmem] * 4,
+        out_specs=in_vmem,
         scratch_shapes=[block((tokens, model)) for _ in range(5)],
         compiler_params=pltpu.CompilerParams(vmem_limit_bytes=32 * 1024 * 1024),
         name="tokens",
-    )(
-        gathered.reshape(tokens, model),
-        ln_gain.reshape(1, model),
-        q_gain.reshape(1, HEAD_DIM),
-        k_gain.reshape(1, HEAD_DIM),
-        w_qkv,
-        w_out,
-    )
+    )(gathered.reshape(tokens, model), gains, wqkv_held, wout_held)
     return exchange(result.reshape(device_count, per_peer, model)).reshape(latent.shape)
 
 

time: 44.4 us -> 41.1 us (0.926)
  waiting for transfers between devices: 9.87 us -> 3.41 us
  Pallas kernels: 5.51 us -> 9.49 us
  local copies, waits for them, and re-layouts: 7.74 us -> 7.06 us
    all_to_all x1, waiting for transfers between devices: 9.87 us -> 3.41 us  [body(): gathered = exchange(latent.reshape(device_count, per_peer, model))]
    pallas_call x0 -> x1, Pallas kernels: none -> 4.06 us  [body(): pl.pallas_call(weights_kernel, out_shape=(pltpu.VMEM((8, model), jnp.floa...]
    reshape x1 -> x0, local copies, waits for them, and re-layouts: 0.7 us -> none  [body(): ln_gain.reshape(1, model)]
    unnamed x9 -> x5, local copies, waits for them, and re-layouts: 7.03 us -> 7.06 us
  transfers between devices with their start and end apart: 1 -> 1, of which waited for: 1 -> 1; matrix products, arithmetic and copies ran while one was open for 2% -> 0% of each run, Pallas kernels for 0% -> 10%
where the time goes in v2:
time: 41.1 us; the launch traced here: 40.9 us
  blocking collectives  13.5 us (33%)
  Pallas kernels  9.49 us (23%)
  starting transfers between devices  7.38 us (18%)
  local copies, waits for them, and re-layouts  7.06 us (17%)
  waiting for transfers between devices  3.41 us (8%)
    all_to_all x1, blocking collectives, body(): exchange(result.reshape(device_count, per_peer, model))  13.5 us
    all_to_all x1, starting transfers between devices, body(): gathered = exchange(latent.reshape(device_count, per_peer, model))  7.38 us
    unnamed x5, local copies, waits for them, and re-layouts  7.06 us
    pallas_call x1, Pallas kernels, body(): pl.pallas_call(functools.partial(tokens_kernel, per_peer), out_shape=jax....  5.43 us
    pallas_call x1, Pallas kernels, body(): pl.pallas_call(weights_kernel, out_shape=(pltpu.VMEM((8, model), jnp.floa...  4.06 us
    all_to_all x1, waiting for transfers between devices, body(): gathered = exchange(latent.reshape(device_count, per_peer, model))  3.41 us
  transfers between devices with their start and end apart: 1, of which 1 were waited for; matrix products, arithmetic and copies ran while one was open for 0% of the time, Pallas kernels for 10%

profile of v2, /device:TPU:0, one launch (start us, length us, event | category | flops | bytes accessed | tf_op | source)
XLA Modules:
  0.0 40.9 jit_solution(7241418567426285037)
XLA Ops:
  0.0 7.4 %all-to-all-start = ((bf16[16,8,1152]{2,1,0:T(8,128)(2,1)}), bf16[16,8,1152]{2,1,0:T(8,128)(2,1)S(1)}, u32[]{:S(2)}, u32[]{:S(2)}) async-start(bf16[16,8,1152]{2,1,0:T(8,128)(2,1)} %bitcast.7), calls=%async_computation | async-start | bytes 589824 | tf_op jit(solution)/shard_map/all_to_all | solution.py:137
  7.4 4.1 %weights.1 = (f32[8,1152]{1,0:T(8,128)S(1)}, bf16[1152,3456]{1,0:T(8,128)(2,1)S(1)}, bf16[1152,1152]{1,0:T(8,128)(2,1)S(1)}) custom-call(f32[1152]{0:T(1024)} %ln_ref.1, f32[72]{0:T(128)} %qg_ref.1, f32[72]{0:T(128)} %kg_ref.1, bf16[1152,3456]{1,0:T(8,128)(2,1)} %wqkv_ref.1, bf16[1152,1152]{1,0:T(8,128)(2,1)} %wout_ref.1), custom_call_target="tpu_custom_call" | custom-call | bytes 21233664 | tf_op jit(solution)/shard_map/weights/pallas_call | solution.py:116
  11.5 0.0 copy-start
  11.5 3.1 %copy-done = bf16[1152,3456]{1,0:T(8,128)(2,1)} copy-done((bf16[1152,3456]{1,0:T(8,128)(2,1)}, bf16[1152,3456]{1,0:T(8,128)(2,1)S(1)}, u32[]{:S(2)}) %copy-start) | copy-done | bytes 7962648
  14.6 3.4 %all-to-all-done = bf16[16,8,1152]{2,1,0:T(8,128)(2,1)S(1)} async-done(((bf16[16,8,1152]{2,1,0:T(8,128)(2,1)}), bf16[16,8,1152]{2,1,0:T(8,128)(2,1)S(1)}, u32[]{:S(2)}, u32[]{:S(2)}) %all-to-all-start) | async-done | bytes 294944 | tf_op jit(solution)/shard_map/all_to_all | solution.py:137
  18.0 0.0 copy-start.1
  18.0 3.3 %copy-done.1 = bf16[1152,3456]{1,0:T(8,128)(2,1)S(1)} copy-done((bf16[1152,3456]{1,0:T(8,128)(2,1)S(1)}, bf16[1152,3456]{1,0:T(8,128)(2,1)}, u32[]{:S(2)}) %copy-start.1) | copy-done | bytes 7962648
  21.2 5.4 %tokens.1 = bf16[128,1152]{1,0:T(8,128)(2,1)S(1)} custom-call(bf16[128,1152]{1,0:T(8,128)(2,1)S(1)} %bitcast.4, f32[8,1152]{1,0:T(8,128)S(1)} %get-tuple-element.8.gains_ref, bf16[1152,3456]{1,0:T(8,128)(2,1)S(1)} %copy-done.1, bf16[1152,1152]{1,0:T(8,128)(2,1)S(1)} %get-tuple-element.10.wout_ref), custom_call_target="tpu_custom_call" | custom-call | tf_op jit(solution)/shard_map/tokens/pallas_call | solution.py:139
  26.7 13.5 %all_to_all.10 = bf16[16,8,1152]{2,1,0:T(8,128)(2,1)S(1)} all-to-all(bf16[16,8,1152]{2,1,0:T(8,128)(2,1)S(1)} %bitcast.5), channel_id=1, replica_groups=mesh['groups'=2,'frame'=16] {'frame'}, dimensions={0} | all-to-all | bytes 589824 | tf_op jit(solution)/shard_map/all_to_all | solution.py:148
  40.2 0.7 %copy.8 = bf16[4,32,1152]{2,1,0:T(8,128)(2,1)} copy(bf16[4,32,1152]{2,1,0:T(8,128)(2,1)S(1)} %bitcast.6) | data formatting | bytes 589824
Async XLA Ops:
  0.0 18.0 %all-to-all-start = ((bf16[16,8,1152]{2,1,0:T(8,128)(2,1)}), bf16[16,8,1152]{2,1,0:T(8,128)(2,1)S(1)}, u32[]{:S(2)}, u32[]{:S(2)}) async-start(bf16[16,8,1152]{2,1,0:T(8,128)(2,1)} %bitcast.7), calls=%async_computation | async-start | bytes 589824 | tf_op jit(solution)/shard_map/all_to_all | solution.py:137
  11.5 3.1 %copy-start = (bf16[1152,3456]{1,0:T(8,128)(2,1)}, bf16[1152,3456]{1,0:T(8,128)(2,1)S(1)}, u32[]{:S(2)}) copy-start(bf16[1152,3456]{1,0:T(8,128)(2,1)S(1)} %get-tuple-element.9.wqkv_ref) | copy-start | bytes 23887876
  18.0 3.3 %copy-start.1 = (bf16[1152,3456]{1,0:T(8,128)(2,1)S(1)}, bf16[1152,3456]{1,0:T(8,128)(2,1)}, u32[]{:S(2)}) copy-start(bf16[1152,3456]{1,0:T(8,128)(2,1)} %copy-done) | copy-start | bytes 23887876

commit v3 on v1

v3 whole, which is shorter than its diff:
```python
import functools

import jax
import jax.numpy as jnp
from jax import lax
from jax.experimental import pallas as pl
from jax.experimental.pallas import tpu as pltpu
from jax.sharding import PartitionSpec as P

HEADS = 16
HEAD_DIM = 72
LANES = 128
EPS = 1e-06


def dot(a, b):
    return jnp.dot(a, b, preferred_element_type=jnp.float32)


def tokens_kernel(
    x_ref,
    ln_hbm,
    qg_hbm,
    kg_hbm,
    wqkv_hbm,
    wout_hbm,
    o_ref,
    wqkv,
    wout,
    ln_ref,
    qg_ref,
    kg_ref,
    normed,
    mixed,
    queries,
    keys,
    values,
    attended,
    sems,
):
    frames, positions, width = x_ref.shape
    tokens = frames * positions
    bf16, f32 = jnp.bfloat16, jnp.float32

    cut = width // 2 // LANES * LANES
    bounds = [(0, cut), (cut, width), (width, 2 * width), (2 * width, 3 * width)]
    pairs = [(ln_hbm, ln_ref), (qg_hbm, qg_ref), (kg_hbm, kg_ref)]
    pairs += [(wqkv_hbm.at[:, pl.ds(a, b - a)], wqkv.at[:, pl.ds(a, b - a)]) for a, b in bounds]
    pairs += [(wout_hbm, wout)]
    copies = [pltpu.make_async_copy(src, dst, sems.at[i]) for i, (src, dst) in enumerate(pairs)]
    for copy in copies:
        copy.start()

    def member_of(feature, lane):
        head = jnp.where(lane >= HEADS, lane - HEADS, lane)
        first = head * HEAD_DIM
        held = (feature >= first) & (feature < first + HEAD_DIM) & (lane < 2 * HEADS)
        return held.astype(f32).astype(bf16)

    shape = (width, LANES)
    member = member_of(lax.broadcasted_iota(jnp.int32, shape, 0), lax.broadcasted_iota(jnp.int32, shape, 1))
    shape = (LANES, width)
    spread_out = member_of(lax.broadcasted_iota(jnp.int32, shape, 1), lax.broadcasted_iota(jnp.int32, shape, 0))

    for copy in copies[:3]:
        copy.wait()
    gain = ln_ref[...].reshape(1, width)
    step = max(1, 16 // positions)
    for frame in range(0, frames, step):
        x = x_ref[frame : frame + step].astype(f32).reshape(step * positions, width)
        center = x - jnp.mean(x, axis=-1, keepdims=True)
        spread = jnp.mean(center * center, axis=-1, keepdims=True)
        rows = slice(frame * positions, (frame + step) * positions)
        normed[rows, :] = (center * lax.rsqrt(spread + EPS) * gain).astype(bf16)

    for copy, (a, b) in zip(copies[3:6], bounds):
        copy.wait()
        part = a // width
        mixed[part * tokens : (part + 1) * tokens, a - part * width : b - part * width] = dot(
            normed[...], wqkv[:, a:b]
        )
    total = dot((mixed[...] * mixed[...]).astype(bf16), member)
    inverse = lax.rsqrt(total * (1.0 / HEAD_DIM) + EPS)
    high = inverse.astype(bf16)
    low = (inverse - high.astype(f32)).astype(bf16)
    lane = lax.broadcasted_iota(jnp.int32, inverse.shape, 1)
    scale = dot(jnp.where(lane < HEADS, high, low), spread_out)
    for part, (head_gain, out) in enumerate(((qg_ref, queries), (kg_ref, keys))):
        rows = slice(part * tokens, (part + 1) * tokens)
        full_gain = jnp.concatenate([head_gain[...].reshape(1, HEAD_DIM)] * HEADS, axis=1)
        out[...] = (mixed[rows, :] * scale[rows, :] * full_gain).astype(bf16)
    copies[6].wait()
    values[...] = dot(normed[...], wqkv[:, 2 * width :]).astype(bf16)

    place = lax.broadcasted_iota(jnp.int32, (tokens, tokens), 0) % positions
    other = lax.broadcasted_iota(jnp.int32, (tokens, tokens), 1) % positions
    same = place == other
    held = {}
    for head in range(HEADS):
        begin, end = head * HEAD_DIM, (head + 1) * HEAD_DIM
        low, high = begin // LANES, -(-end // LANES)
        window = slice(low * LANES, high * LANES)
        lane = lax.broadcasted_iota(jnp.int32, (1, (high - low) * LANES), 1) + low * LANES
        mine = (lane >= begin) & (lane < end)
        query = jnp.where(mine, queries[:, window], jnp.zeros((), bf16))
        scores = lax.dot_general(
            query, keys[:, window], (((1,), (1,)), ((), ())), preferred_element_type=f32
        ) * HEAD_DIM ** (-0.5)
        weights = jnp.where(same, jnp.exp(scores), 0.0)
        weights = (weights / jnp.sum(weights, axis=-1, keepdims=True)).astype(bf16)
        value = jnp.where(mine, values[:, window], jnp.zeros((), bf16))
        heads_out = dot(weights, value)
        for tile in range(low, high):
            piece = heads_out[:, (tile - low) * LANES : (tile - low + 1) * LANES]
            held[tile] = held[tile] + piece if tile in held else piece
            if end >= (tile + 1) * LANES:
                attended[:, tile * LANES : (tile + 1) * LANES] = held.pop(tile).astype(bf16)

    copies[7].wait()
    branch = dot(attended[...], wout[...])
    o_ref[...] = (x_ref[...].astype(f32) + branch.reshape(x_ref.shape)).astype(bf16)


def body(latent, ln_gain, q_gain, k_gain, w_qkv, w_out):
    device_count = lax.axis_size("frame")
    rows, columns, model = latent.shape
    tokens = rows * columns
    per_peer = tokens // device_count
    exchange = functools.partial(
        lax.all_to_all, axis_name="frame", split_axis=0, concat_axis=0, tiled=True
    )
    gathered = exchange(latent.reshape(device_count, per_peer, model))
    in_vmem = pl.BlockSpec(memory_space=pltpu.VMEM)
    in_hbm = pl.BlockSpec(memory_space=pltpu.HBM)
    bf16, f32 = jnp.bfloat16, jnp.float32
    result = pl.pallas_call(
        tokens_kernel,
        out_shape=jax.ShapeDtypeStruct(gathered.shape, bf16),
        in_specs=[in_vmem] + [in_hbm] * 5,
        out_specs=in_vmem,
        scratch_shapes=[
            pltpu.VMEM(w_qkv.shape, bf16),
            pltpu.VMEM(w_out.shape, bf16),
            pltpu.VMEM((model,), f32),
            pltpu.VMEM((HEAD_DIM,), f32),
            pltpu.VMEM((HEAD_DIM,), f32),
            pltpu.VMEM((tokens, model), bf16),
            pltpu.VMEM((2 * tokens, model), f32),
            pltpu.VMEM((tokens, model), bf16),
            pltpu.VMEM((tokens, model), bf16),
            pltpu.VMEM((tokens, model), bf16),
            pltpu.VMEM((tokens, model), bf16),
            pltpu.SemaphoreType.DMA((8,)),
        ],
        compiler_params=pltpu.CompilerParams(vmem_limit_bytes=40 * 1024 * 1024),
        name="tokens",
    )(gathered, *(pltpu.with_memory_space_constraint(a, pltpu.HBM) for a in (ln_gain, q_gain, k_gain, w_qkv, w_out)))
    return exchange(result).reshape(latent.shape)


def solution(mesh):
    placed = (P(("groups", "frame"), None, None), P(), P(), P(), P(), P())
    return jax.shard_map(
        body,
        mesh=mesh,
        in_specs=placed,
        out_specs=P(("groups", "frame"), None, None),
        check_vma=False,
    )
```

time: 44.4 us -> 39.4 us (0.89)
  blocking collectives: 13.5 us -> 31.4 us
  waiting for transfers between devices: 9.87 us -> 0 us
  starting transfers between devices: 7.39 us -> 0 us
  local copies, waits for them, and re-layouts: 7.74 us -> 0.71 us
  Pallas kernels: 5.51 us -> 6.97 us
    all_to_all x1 -> x2, blocking collectives: 13.5 us -> 31.4 us  [the longest x1 18 us: body(): gathered = exchange(latent.reshape(device_count, per_peer, model))]
    all_to_all x1 -> x0, waiting for transfers between devices: 9.87 us -> none  [body(): gathered = exchange(latent.reshape(device_count, per_peer, model))]
    all_to_all x1 -> x0, starting transfers between devices: 7.39 us -> none  [body(): gathered = exchange(latent.reshape(device_count, per_peer, model))]
    unnamed x9 -> x1, local copies, waits for them, and re-layouts: 7.03 us -> 0.71 us
    pallas_call x1, Pallas kernels: 5.51 us -> 6.97 us  [body(): pl.pallas_call(tokens_kernel, out_shape=jax.ShapeDtypeStruct(gathered.sha...]
    reshape x1 -> x0, local copies, waits for them, and re-layouts: 0.7 us -> none  [body(): ln_gain.reshape(1, model)]
  transfers between devices with their start and end apart: 1 -> 0, of which waited for: 1 -> 0; matrix products, arithmetic and copies ran while one was open for 2% -> 0% of each run, Pallas kernels for 0% -> 0%
where the time goes in v3:
time: 39.4 us; the launch traced here: 39.1 us
  blocking collectives  31.4 us (80%)
  Pallas kernels  6.97 us (18%)
  local copies, waits for them, and re-layouts  0.71 us (2%)
    all_to_all x1, blocking collectives, body(): gathered = exchange(latent.reshape(device_count, per_peer, model))  18 us
    all_to_all x1, blocking collectives, body(): return exchange(result).reshape(latent.shape)  13.5 us
    pallas_call x1, Pallas kernels, body(): pl.pallas_call(tokens_kernel, out_shape=jax.ShapeDtypeStruct(gathered.sha...  6.97 us

profile of v3, /device:TPU:0, one launch (start us, length us, event | category | flops | bytes accessed | tf_op | source)
XLA Modules:
  0.0 39.1 jit_solution(2746634068028045267)
XLA Ops:
  0.0 18.0 %all_to_all.10.x_ref = bf16[16,8,1152]{2,1,0:T(8,128)(2,1)S(1)} all-to-all(bf16[16,8,1152]{2,1,0:T(8,128)(2,1)} %bitcast.3), channel_id=1, replica_groups=mesh['groups'=2,'frame'=16] {'frame'}, dimensions={0} | all-to-all | bytes 589824 | tf_op jit(solution)/shard_map/all_to_all | solution.py:132
  18.0 7.0 %tokens.1 = bf16[16,8,1152]{2,1,0:T(8,128)(2,1)S(1)} custom-call(bf16[16,8,1152]{2,1,0:T(8,128)(2,1)S(1)} %all_to_all.10.x_ref, f32[1152]{0:T(1024)} %ln_hbm.1, f32[72]{0:T(128)} %qg_hbm.1, f32[72]{0:T(128)} %kg_hbm.1, bf16[1152,3456]{1,0:T(8,128)(2,1)} %wqkv_hbm.1, bf16[1152,1152]{1,0:T(8,128)(2,1)} %wout_hbm.1), custom_call_target="tpu_custom_call" | custom-call | tf_op jit(solution)/shard_map/tokens/pallas_call | solution.py:136
  24.9 13.5 %all_to_all.11 = bf16[16,8,1152]{2,1,0:T(8,128)(2,1)S(1)} all-to-all(bf16[16,8,1152]{2,1,0:T(8,128)(2,1)S(1)} %tokens.1), channel_id=1, replica_groups=mesh['groups'=2,'frame'=16] {'frame'}, dimensions={0} | all-to-all | bytes 589824 | tf_op jit(solution)/shard_map/all_to_all | solution.py:158
  38.4 0.7 %copy.8 = bf16[4,32,1152]{2,1,0:T(8,128)(2,1)} copy(bf16[4,32,1152]{2,1,0:T(8,128)(2,1)S(1)} %bitcast.2) | data formatting | bytes 589824

commit v4 on v3

--- a/solution.py
+++ b/solution.py
@@ -17,29 +17,11 @@
     return jnp.dot(a, b, preferred_element_type=jnp.float32)
 
 
-def tokens_kernel(
-    x_ref,
-    ln_hbm,
-    qg_hbm,
-    kg_hbm,
-    wqkv_hbm,
-    wout_hbm,
-    o_ref,
-    wqkv,
-    wout,
-    ln_ref,
-    qg_ref,
-    kg_ref,
-    normed,
-    mixed,
-    queries,
-    keys,
-    values,
-    attended,
-    sems,
-):
+def tokens_kernel(x_ref, ln_hbm, qg_hbm, kg_hbm, wqkv_hbm, wout_hbm, *refs):
     frames, positions, width = x_ref.shape
     tokens = frames * positions
+    slabs = refs[:frames]
+    wqkv, wout, ln_ref, qg_ref, kg_ref, normed, mixed, queries, keys, values, attended, result, sems = refs[frames:]
     bf16, f32 = jnp.bfloat16, jnp.float32
 
     cut = width // 2 // LANES * LANES
@@ -79,7 +61,10 @@
         mixed[part * tokens : (part + 1) * tokens, a - part * width : b - part * width] = dot(
             normed[...], wqkv[:, a:b]
         )
-    total = dot((mixed[...] * mixed[...]).astype(bf16), member)
+    squares = mixed[...] * mixed[...]
+    high = squares.astype(bf16)
+    low = (squares - high.astype(f32)).astype(bf16)
+    total = dot(high, member) + dot(low, member)
     inverse = lax.rsqrt(total * (1.0 / HEAD_DIM) + EPS)
     high = inverse.astype(bf16)
     low = (inverse - high.astype(f32)).astype(bf16)
@@ -118,7 +103,24 @@
 
     copies[7].wait()
     branch = dot(attended[...], wout[...])
-    o_ref[...] = (x_ref[...].astype(f32) + branch.reshape(x_ref.shape)).astype(bf16)
+    result[...] = (x_ref[...].astype(f32) + branch.reshape(x_ref.shape)).astype(bf16)
+    me = lax.axis_index("frame")
+    for k, slab in enumerate(slabs):
+        slab[...] = result[lax.rem(me + k, frames)]
+
+
+def ordered_kernel(*refs):
+    slabs, out, sems = refs[:-2], refs[-2], refs[-1]
+    count = len(slabs)
+    me = lax.axis_index("frame")
+    copies = [
+        pltpu.make_async_copy(slab, out.at[lax.rem(me + count - k, count)], sems.at[k])
+        for k, slab in enumerate(slabs)
+    ]
+    for copy in copies:
+        copy.start()
+    for copy in copies:
+        copy.wait()
 
 
 def body(latent, ln_gain, q_gain, k_gain, w_qkv, w_out):
@@ -133,11 +135,11 @@
     in_vmem = pl.BlockSpec(memory_space=pltpu.VMEM)
     in_hbm = pl.BlockSpec(memory_space=pltpu.HBM)
     bf16, f32 = jnp.bfloat16, jnp.float32
-    result = pl.pallas_call(
+    slabs = pl.pallas_call(
         tokens_kernel,
-        out_shape=jax.ShapeDtypeStruct(gathered.shape, bf16),
+        out_shape=[jax.ShapeDtypeStruct((per_peer, model), bf16)] * device_count,
         in_specs=[in_vmem] + [in_hbm] * 5,
-        out_specs=in_vmem,
+        out_specs=[in_vmem] * device_count,
         scratch_shapes=[
             pltpu.VMEM(w_qkv.shape, bf16),
             pltpu.VMEM(w_out.shape, bf16),
@@ -150,12 +152,25 @@
             pltpu.VMEM((tokens, model), bf16),
             pltpu.VMEM((tokens, model), bf16),
             pltpu.VMEM((tokens, model), bf16),
+            pltpu.VMEM(gathered.shape, bf16),
             pltpu.SemaphoreType.DMA((8,)),
         ],
         compiler_params=pltpu.CompilerParams(vmem_limit_bytes=40 * 1024 * 1024),
         name="tokens",
     )(gathered, *(pltpu.with_memory_space_constraint(a, pltpu.HBM) for a in (ln_gain, q_gain, k_gain, w_qkv, w_out)))
-    return exchange(result).reshape(latent.shape)
+    arrived = [slabs[0]]
+    for k in range(1, device_count):
+        ahead = [(i, (i + k) % device_count) for i in range(device_count)]
+        arrived.append(lax.ppermute(slabs[k], "frame", ahead))
+    result = pl.pallas_call(
+        ordered_kernel,
+        out_shape=pltpu.HBM(gathered.shape, bf16),
+        in_specs=[pl.BlockSpec(memory_space=pl.ANY)] * device_count,
+        out_specs=in_hbm,
+        scratch_shapes=[pltpu.SemaphoreType.DMA((device_count,))],
+        name="ordered",
+    )(*arrived)
+    return result.reshape(latent.shape)
 
 
 def solution(mesh):

time: 39.4 us -> 59.7 us (1.52)
  starting transfers between devices: 0 us -> 18.5 us
  blocking collectives: 31.4 us -> 18 us
  Pallas kernels: 6.97 us -> 17.6 us
  waiting for transfers between devices: 0 us -> 4.23 us
    ppermute x0 -> x15, starting transfers between devices: none -> 18.5 us  [body(): arrived.append(lax.ppermute(slabs[k], 'frame', ahead))]
    all_to_all x1 -> x0, blocking collectives: 13.5 us -> none  [body(): return exchange(result).reshape(latent.shape)]
    pallas_call x1 -> x2, Pallas kernels: 6.97 us -> 17.6 us  [the longest x1 10.2 us: body(): pl.pallas_call(ordered_kernel, out_shape=pltpu.HBM(gathered.shape, bf16),...]
    ppermute x0 -> x15, waiting for transfers between devices: none -> 4.23 us  [body(): arrived.append(lax.ppermute(slabs[k], 'frame', ahead))]
  transfers between devices with their start and end apart: 0 -> 15, of which waited for: 0 -> 2; matrix products, arithmetic and copies ran while one was open for 0% -> 0% of each run, Pallas kernels for 0% -> 0%
where the time goes in v4:
time: 59.7 us; the launch traced here: 59.5 us
  starting transfers between devices  18.5 us (31%)
  blocking collectives  18 us (30%)
  Pallas kernels  17.6 us (29%)
  waiting for transfers between devices  4.23 us (7%)
  local copies, waits for them, and re-layouts  1.13 us (2%)
    ppermute x15, starting transfers between devices, body(): arrived.append(lax.ppermute(slabs[k], 'frame', ahead))  18.5 us
    all_to_all x1, blocking collectives, body(): gathered = exchange(latent.reshape(device_count, per_peer, model))  18 us
    pallas_call x1, Pallas kernels, body(): pl.pallas_call(ordered_kernel, out_shape=pltpu.HBM(gathered.shape, bf16),...  10.2 us
    pallas_call x1, Pallas kernels, body(): pl.pallas_call(tokens_kernel, out_shape=[jax.ShapeDtypeStruct((per_peer,...  7.4 us
    ppermute x15, waiting for transfers between devices, body(): arrived.append(lax.ppermute(slabs[k], 'frame', ahead))  4.23 us
  transfers between devices with their start and end apart: 15, of which 2 were waited for; matrix products, arithmetic and copies ran while one was open for 0% of the time, Pallas kernels for 0%

profile of v4, /device:TPU:0, one launch (start us, length us, event | category | flops | bytes accessed | tf_op | source)
XLA Modules:
  0.0 59.5 jit_solution(6733051767610720619)
XLA Ops:
  0.0 18.0 %all_to_all.5.x_ref = bf16[16,8,1152]{2,1,0:T(8,128)(2,1)S(1)} all-to-all(bf16[16,8,1152]{2,1,0:T(8,128)(2,1)} %bitcast.2), channel_id=1, replica_groups=mesh['groups'=2,'frame'=16] {'frame'}, dimensions={0} | all-to-all | bytes 589824 | tf_op jit(solution)/shard_map/all_to_all | solution.py:134
  18.0 7.4 %tokens.1 = (bf16[8,1152]{1,0:T(8,128)(2,1)S(1)}, bf16[8,1152]{1,0:T(8,128)(2,1)S(1)}, bf16[8,1152]{1,0:T(8,128)(2,1)S(1)}, bf16[8,1152]{1,0:T(8,128)(2,1)S(1)},...) custom-call(bf16[16,8,1152]{2,1,0:T(8,128)(2,1)S(1)} %all_to_all.5.x, ...), custom_call_target="tpu_custom_call" | custom-call | tf_op jit(solution)/shard_map/tokens/pallas_call | solution.py:138
  25.4 0.0 copy-start
  25.4 0.6 copy-done
  26.0 0.0 collective-permute-start
  26.0 0.7 %collective-permute-start.1 = (bf16[8,1152]{1,0:T(8,128)(2,1)S(1)}, bf16[8,1152]{1,0:T(8,128)(2,1)S(1)}, u32[]{:S(2)}, u32[]{:S(2)}) collective-permute-start(bf16[8,1152]{1,0:T(8,128)(2,1)S(1)} %get-tuple-element.23), channel_id=1, source_target_pairs={{0,2},{1,3},{2,4},{3,5},{4,6},{5,7},{6,8},{7,9},{8,10},{9,11},{10,... | collective-permute-start | bytes 55304 | tf_op jit(solution)/shard_map/ppermute | solution.py:164
  26.6 1.6 %collective-permute-start.2 = (bf16[8,1152]{1,0:T(8,128)(2,1)S(1)}, bf16[8,1152]{1,0:T(8,128)(2,1)S(1)}, u32[]{:S(2)}, u32[]{:S(2)}) collective-permute-start(bf16[8,1152]{1,0:T(8,128)(2,1)S(1)} %get-tuple-element.24), channel_id=1, source_target_pairs={{0,3},{1,4},{2,5},{3,6},{4,7},{5,8},{6,9},{7,10},{8,11},{9,12},{10... | collective-permute-start | bytes 55304 | tf_op jit(solution)/shard_map/ppermute | solution.py:164
  28.2 0.8 %collective-permute-start.3 = (bf16[8,1152]{1,0:T(8,128)(2,1)S(1)}, bf16[8,1152]{1,0:T(8,128)(2,1)S(1)}, u32[]{:S(2)}, u32[]{:S(2)}) collective-permute-start(bf16[8,1152]{1,0:T(8,128)(2,1)S(1)} %get-tuple-element.25), channel_id=1, source_target_pairs={{0,4},{1,5},{2,6},{3,7},{4,8},{5,9},{6,10},{7,11},{8,12},{9,13},{1... | collective-permute-start | bytes 55304 | tf_op jit(solution)/shard_map/ppermute | solution.py:164
  29.0 0.1 collective-permute-start.4
  29.1 2.8 %collective-permute-done.refs_1_ = bf16[8,1152]{1,0:T(8,128)(2,1)S(1)} collective-permute-done((bf16[8,1152]{1,0:T(8,128)(2,1)S(1)}, bf16[8,1152]{1,0:T(8,128)(2,1)S(1)}, u32[]{:S(2)}, u32[]{:S(2)}) %collective-permute-start) | collective-permute-done | bytes 18464 | tf_op jit(solution)/shard_map/ppermute | solution.py:164
  31.8 0.9 %collective-permute-start.5 = (bf16[8,1152]{1,0:T(8,128)(2,1)S(1)}, bf16[8,1152]{1,0:T(8,128)(2,1)S(1)}, u32[]{:S(2)}, u32[]{:S(2)}) collective-permute-start(bf16[8,1152]{1,0:T(8,128)(2,1)S(1)} %get-tuple-element.27), channel_id=1, source_target_pairs={{0,6},{1,7},{2,8},{3,9},{4,10},{5,11},{6,12},{7,13},{8,14},{9,15},... | collective-permute-start | bytes 55304 | tf_op jit(solution)/shard_map/ppermute | solution.py:164
  32.8 0.0 collective-permute-done.1.refs_2_
  32.8 1.9 %collective-permute-start.6 = (bf16[8,1152]{1,0:T(8,128)(2,1)S(1)}, bf16[8,1152]{1,0:T(8,128)(2,1)S(1)}, u32[]{:S(2)}, u32[]{:S(2)}) collective-permute-start(bf16[8,1152]{1,0:T(8,128)(2,1)S(1)} %get-tuple-element.28), channel_id=1, source_target_pairs={{0,7},{1,8},{2,9},{3,10},{4,11},{5,12},{6,13},{7,14},{8,15},{9,0},... | collective-permute-start | bytes 55304 | tf_op jit(solution)/shard_map/ppermute | solution.py:164
  34.7 0.0 collective-permute-done.2.refs_3_
  34.7 1.5 %collective-permute-start.7 = (bf16[8,1152]{1,0:T(8,128)(2,1)S(1)}, bf16[8,1152]{1,0:T(8,128)(2,1)S(1)}, u32[]{:S(2)}, u32[]{:S(2)}) collective-permute-start(bf16[8,1152]{1,0:T(8,128)(2,1)S(1)} %get-tuple-element.29), channel_id=1, source_target_pairs={{0,8},{1,9},{2,10},{3,11},{4,12},{5,13},{6,14},{7,15},{8,0},{9,1},... | collective-permute-start | bytes 55304 | tf_op jit(solution)/shard_map/ppermute | solution.py:164
  36.2 0.0 collective-permute-done.3.refs_4_
  36.2 0.2 collective-permute-start.8
  36.4 0.0 collective-permute-done.4.refs_5_
  36.4 2.3 %collective-permute-start.9 = (bf16[8,1152]{1,0:T(8,128)(2,1)S(1)}, bf16[8,1152]{1,0:T(8,128)(2,1)S(1)}, u32[]{:S(2)}, u32[]{:S(2)}) collective-permute-start(bf16[8,1152]{1,0:T(8,128)(2,1)S(1)} %get-tuple-element.31), channel_id=1, source_target_pairs={{0,10},{1,11},{2,12},{3,13},{4,14},{5,15},{6,0},{7,1},{8,2},{9,3},... | collective-permute-start | bytes 55304 | tf_op jit(solution)/shard_map/ppermute | solution.py:164
  38.7 0.0 collective-permute-done.5.refs_6_
  38.7 3.2 %collective-permute-start.10 = (bf16[8,1152]{1,0:T(8,128)(2,1)S(1)}, bf16[8,1152]{1,0:T(8,128)(2,1)S(1)}, u32[]{:S(2)}, u32[]{:S(2)}) collective-permute-start(bf16[8,1152]{1,0:T(8,128)(2,1)S(1)} %get-tuple-element.32), channel_id=1, source_target_pairs={{0,11},{1,12},{2,13},{3,14},{4,15},{5,0},{6,1},{7,2},{8,3},{9,4},{... | collective-permute-start | bytes 55304 | tf_op jit(solution)/shard_map/ppermute | solution.py:164
  42.0 0.0 collective-permute-done.6.refs_7_
  42.0 0.4 collective-permute-start.11
  42.3 0.0 collective-permute-done.7.refs_8_
  42.3 1.1 %collective-permute-start.12 = (bf16[8,1152]{1,0:T(8,128)(2,1)S(1)}, bf16[8,1152]{1,0:T(8,128)(2,1)S(1)}, u32[]{:S(2)}, u32[]{:S(2)}) collective-permute-start(bf16[8,1152]{1,0:T(8,128)(2,1)S(1)} %get-tuple-element.34), channel_id=1, source_target_pairs={{0,13},{1,14},{2,15},{3,0},{4,1},{5,2},{6,3},{7,4},{8,5},{9,6},{10... | collective-permute-start | bytes 55304 | tf_op jit(solution)/shard_map/ppermute | solution.py:164
  43.5 0.0 collective-permute-done.8.refs_9_
  43.5 1.3 %collective-permute-start.13 = (bf16[8,1152]{1,0:T(8,128)(2,1)S(1)}, bf16[8,1152]{1,0:T(8,128)(2,1)S(1)}, u32[]{:S(2)}, u32[]{:S(2)}) collective-permute-start(bf16[8,1152]{1,0:T(8,128)(2,1)S(1)} %get-tuple-element.35), channel_id=1, source_target_pairs={{0,14},{1,15},{2,0},{3,1},{4,2},{5,3},{6,4},{7,5},{8,6},{9,7},{10,... | collective-permute-start | bytes 55304 | tf_op jit(solution)/shard_map/ppermute | solution.py:164
  44.7 0.0 collective-permute-done.9.refs_10_
  44.7 2.5 %collective-permute-start.14 = (bf16[8,1152]{1,0:T(8,128)(2,1)S(1)}, bf16[8,1152]{1,0:T(8,128)(2,1)S(1)}, u32[]{:S(2)}, u32[]{:S(2)}) collective-permute-start(bf16[8,1152]{1,0:T(8,128)(2,1)S(1)} %get-tuple-element.36), channel_id=1, source_target_pairs={{0,15},{1,0},{2,1},{3,2},{4,3},{5,4},{6,5},{7,6},{8,7},{9,8},{10,9... | collective-permute-start | bytes 55304 | tf_op jit(solution)/shard_map/ppermute | solution.py:164
  47.3 0.0 collective-permute-done.10.refs_11_
  47.3 0.0 collective-permute-done.11.refs_12_
  47.3 0.0 copy-start.12
  47.3 0.0 collective-permute-done.12.refs_13_
  47.3 0.0 copy-start.13
  47.3 0.0 collective-permute-done.13.refs_14_
  47.3 0.0 copy-start.14
  47.4 1.4 %collective-permute-done.14.refs_15_ = bf16[8,1152]{1,0:T(8,128)(2,1)S(1)} collective-permute-done((bf16[8,1152]{1,0:T(8,128)(2,1)S(1)}, bf16[8,1152]{1,0:T(8,128)(2,1)S(1)}, u32[]{:S(2)}, u32[]{:S(2)}) %collective-permute-start.14) | collective-permute-done | bytes 18464 | tf_op jit(solution)/shard_map/ppermute | solution.py:164
  48.8 0.0 copy-done.1
  48.8 0.0 copy-done.2
  48.8 0.0 copy-done.3
  48.8 0.0 copy-done.4
  48.8 0.0 copy-done.5
  48.8 0.0 copy-done.6
  48.8 0.0 copy-done.7
  48.8 0.0 copy-done.8
  48.8 0.0 copy-done.9
  48.9 0.5 copy-done.15
  49.4 10.2 %ordered.1 = bf16[16,8,1152]{2,1,0:T(8,128)(2,1)} custom-call(bf16[8,1152]{1,0:T(8,128)(2,1)} %copy-done, bf16[8,1152]{1,0:T(8,128)(2,1)} %copy-done.1, bf16[8,1152]{1,0:T(8,128)(2,1)} %copy-done.2, bf16[8,1152]{1,0:T(8,128)(2,1)} %copy-done.3, bf16[8,1152]{1,0:T(8,128)(2,1)} %copy-done.4, bf16[8,1152]{1,0:T(8,128)(2,1)} %copy-done.5, ...), custom_call_target="tpu_custom_call" | custom-call | tf_op jit(solution)/shard_map/ordered/pallas_call | solution.py:165
  (17 shorter events, 0.0 us)
Async XLA Ops:
  25.4 0.6 %copy-start = (bf16[8,1152]{1,0:T(8,128)(2,1)}, bf16[8,1152]{1,0:T(8,128)(2,1)S(1)}, u32[]{:S(2)}) copy-start(bf16[8,1152]{1,0:T(8,128)(2,1)S(1)} %get-tuple-element.21.refs_0_) | copy-start | bytes 55300
  26.0 5.9 %collective-permute-start = (bf16[8,1152]{1,0:T(8,128)(2,1)S(1)}, bf16[8,1152]{1,0:T(8,128)(2,1)S(1)}, u32[]{:S(2)}, u32[]{:S(2)}) collective-permute-start(bf16[8,1152]{1,0:T(8,128)(2,1)S(1)} %get-tuple-element.22), channel_id=1, source_target_pairs={{0,1},{1,2},{2,3},{3,4},{4,5},{5,6},{6,7},{7,8},{8,9},{9,10},{10,1... | collective-permute-start | bytes 55304 | tf_op jit(solution)/shard_map/ppermute | solution.py:164
  26.0 6.8 %collective-permute-start.1 = (bf16[8,1152]{1,0:T(8,128)(2,1)S(1)}, bf16[8,1152]{1,0:T(8,128)(2,1)S(1)}, u32[]{:S(2)}, u32[]{:S(2)}) collective-permute-start(bf16[8,1152]{1,0:T(8,128)(2,1)S(1)} %get-tuple-element.23), channel_id=1, source_target_pairs={{0,2},{1,3},{2,4},{3,5},{4,6},{5,7},{6,8},{7,9},{8,10},{9,11},{10,... | collective-permute-start | bytes 55304 | tf_op jit(solution)/shard_map/ppermute | solution.py:164
  26.6 8.1 %collective-permute-start.2 = (bf16[8,1152]{1,0:T(8,128)(2,1)S(1)}, bf16[8,1152]{1,0:T(8,128)(2,1)S(1)}, u32[]{:S(2)}, u32[]{:S(2)}) collective-permute-start(bf16[8,1152]{1,0:T(8,128)(2,1)S(1)} %get-tuple-element.24), channel_id=1, source_target_pairs={{0,3},{1,4},{2,5},{3,6},{4,7},{5,8},{6,9},{7,10},{8,11},{9,12},{10... | collective-permute-start | bytes 55304 | tf_op jit(solution)/shard_map/ppermute | solution.py:164
  28.2 8.0 %collective-permute-start.3 = (bf16[8,1152]{1,0:T(8,128)(2,1)S(1)}, bf16[8,1152]{1,0:T(8,128)(2,1)S(1)}, u32[]{:S(2)}, u32[]{:S(2)}) collective-permute-start(bf16[8,1152]{1,0:T(8,128)(2,1)S(1)} %get-tuple-element.25), channel_id=1, source_target_pairs={{0,4},{1,5},{2,6},{3,7},{4,8},{5,9},{6,10},{7,11},{8,12},{9,13},{1... | collective-permute-start | bytes 55304 | tf_op jit(solution)/shard_map/ppermute | solution.py:164
  29.0 7.4 %collective-permute-start.4 = (bf16[8,1152]{1,0:T(8,128)(2,1)S(1)}, bf16[8,1152]{1,0:T(8,128)(2,1)S(1)}, u32[]{:S(2)}, u32[]{:S(2)}) collective-permute-start(bf16[8,1152]{1,0:T(8,128)(2,1)S(1)} %get-tuple-element.26), channel_id=1, source_target_pairs={{0,5},{1,6},{2,7},{3,8},{4,9},{5,10},{6,11},{7,12},{8,13},{9,14},{... | collective-permute-start | bytes 55304 | tf_op jit(solution)/shard_map/ppermute | solution.py:164
  31.8 16.9 %copy-start.1 = (bf16[8,1152]{1,0:T(8,128)(2,1)}, bf16[8,1152]{1,0:T(8,128)(2,1)S(1)}, u32[]{:S(2)}) copy-start(bf16[8,1152]{1,0:T(8,128)(2,1)S(1)} %collective-permute-done.refs_1_) | copy-start | bytes 55300
  31.8 6.9 %collective-permute-start.5 = (bf16[8,1152]{1,0:T(8,128)(2,1)S(1)}, bf16[8,1152]{1,0:T(8,128)(2,1)S(1)}, u32[]{:S(2)}, u32[]{:S(2)}) collective-permute-start(bf16[8,1152]{1,0:T(8,128)(2,1)S(1)} %get-tuple-element.27), channel_id=1, source_target_pairs={{0,6},{1,7},{2,8},{3,9},{4,10},{5,11},{6,12},{7,13},{8,14},{9,15},... | collective-permute-start | bytes 55304 | tf_op jit(solution)/shard_map/ppermute | solution.py:164
  32.8 16.0 %copy-start.2 = (bf16[8,1152]{1,0:T(8,128)(2,1)}, bf16[8,1152]{1,0:T(8,128)(2,1)S(1)}, u32[]{:S(2)}) copy-start(bf16[8,1152]{1,0:T(8,128)(2,1)S(1)} %collective-permute-done.1.refs_2_) | copy-start | bytes 55300
  32.8 9.2 %collective-permute-start.6 = (bf16[8,1152]{1,0:T(8,128)(2,1)S(1)}, bf16[8,1152]{1,0:T(8,128)(2,1)S(1)}, u32[]{:S(2)}, u32[]{:S(2)}) collective-permute-start(bf16[8,1152]{1,0:T(8,128)(2,1)S(1)} %get-tuple-element.28), channel_id=1, source_target_pairs={{0,7},{1,8},{2,9},{3,10},{4,11},{5,12},{6,13},{7,14},{8,15},{9,0},... | collective-permute-start | bytes 55304 | tf_op jit(solution)/shard_map/ppermute | solution.py:164
  34.7 14.1 %copy-start.3 = (bf16[8,1152]{1,0:T(8,128)(2,1)}, bf16[8,1152]{1,0:T(8,128)(2,1)S(1)}, u32[]{:S(2)}) copy-start(bf16[8,1152]{1,0:T(8,128)(2,1)S(1)} %collective-permute-done.2.refs_3_) | copy-start | bytes 55300
  34.7 7.6 %collective-permute-start.7 = (bf16[8,1152]{1,0:T(8,128)(2,1)S(1)}, bf16[8,1152]{1,0:T(8,128)(2,1)S(1)}, u32[]{:S(2)}, u32[]{:S(2)}) collective-permute-start(bf16[8,1152]{1,0:T(8,128)(2,1)S(1)} %get-tuple-element.29), channel_id=1, source_target_pairs={{0,8},{1,9},{2,10},{3,11},{4,12},{5,13},{6,14},{7,15},{8,0},{9,1},... | collective-permute-start | bytes 55304 | tf_op jit(solution)/shard_map/ppermute | solution.py:164
  36.2 12.6 %copy-start.4 = (bf16[8,1152]{1,0:T(8,128)(2,1)}, bf16[8,1152]{1,0:T(8,128)(2,1)S(1)}, u32[]{:S(2)}) copy-start(bf16[8,1152]{1,0:T(8,128)(2,1)S(1)} %collective-permute-done.3.refs_4_) | copy-start | bytes 55300
  36.2 7.3 %collective-permute-start.8 = (bf16[8,1152]{1,0:T(8,128)(2,1)S(1)}, bf16[8,1152]{1,0:T(8,128)(2,1)S(1)}, u32[]{:S(2)}, u32[]{:S(2)}) collective-permute-start(bf16[8,1152]{1,0:T(8,128)(2,1)S(1)} %get-tuple-element.30), channel_id=1, source_target_pairs={{0,9},{1,10},{2,11},{3,12},{4,13},{5,14},{6,15},{7,0},{8,1},{9,2},... | collective-permute-start | bytes 55304 | tf_op jit(solution)/shard_map/ppermute | solution.py:164
  36.4 12.4 %copy-start.5 = (bf16[8,1152]{1,0:T(8,128)(2,1)}, bf16[8,1152]{1,0:T(8,128)(2,1)S(1)}, u32[]{:S(2)}) copy-start(bf16[8,1152]{1,0:T(8,128)(2,1)S(1)} %collective-permute-done.4.refs_5_) | copy-start | bytes 55300
  36.4 8.3 %collective-permute-start.9 = (bf16[8,1152]{1,0:T(8,128)(2,1)S(1)}, bf16[8,1152]{1,0:T(8,128)(2,1)S(1)}, u32[]{:S(2)}, u32[]{:S(2)}) collective-permute-start(bf16[8,1152]{1,0:T(8,128)(2,1)S(1)} %get-tuple-element.31), channel_id=1, source_target_pairs={{0,10},{1,11},{2,12},{3,13},{4,14},{5,15},{6,0},{7,1},{8,2},{9,3},... | collective-permute-start | bytes 55304 | tf_op jit(solution)/shard_map/ppermute | solution.py:164
  38.7 10.0 %copy-start.6 = (bf16[8,1152]{1,0:T(8,128)(2,1)}, bf16[8,1152]{1,0:T(8,128)(2,1)S(1)}, u32[]{:S(2)}) copy-start(bf16[8,1152]{1,0:T(8,128)(2,1)S(1)} %collective-permute-done.5.refs_6_) | copy-start | bytes 55300
  38.7 8.5 %collective-permute-start.10 = (bf16[8,1152]{1,0:T(8,128)(2,1)S(1)}, bf16[8,1152]{1,0:T(8,128)(2,1)S(1)}, u32[]{:S(2)}, u32[]{:S(2)}) collective-permute-start(bf16[8,1152]{1,0:T(8,128)(2,1)S(1)} %get-tuple-element.32), channel_id=1, source_target_pairs={{0,11},{1,12},{2,13},{3,14},{4,15},{5,0},{6,1},{7,2},{8,3},{9,4},{... | collective-permute-start | bytes 55304 | tf_op jit(solution)/shard_map/ppermute | solution.py:164
  42.0 6.8 %copy-start.7 = (bf16[8,1152]{1,0:T(8,128)(2,1)}, bf16[8,1152]{1,0:T(8,128)(2,1)S(1)}, u32[]{:S(2)}) copy-start(bf16[8,1152]{1,0:T(8,128)(2,1)S(1)} %collective-permute-done.6.refs_7_) | copy-start | bytes 55300
  42.0 5.3 %collective-permute-start.11 = (bf16[8,1152]{1,0:T(8,128)(2,1)S(1)}, bf16[8,1152]{1,0:T(8,128)(2,1)S(1)}, u32[]{:S(2)}, u32[]{:S(2)}) collective-permute-start(bf16[8,1152]{1,0:T(8,128)(2,1)S(1)} %get-tuple-element.33), channel_id=1, source_target_pairs={{0,12},{1,13},{2,14},{3,15},{4,0},{5,1},{6,2},{7,3},{8,4},{9,5},{1... | collective-permute-start | bytes 55304 | tf_op jit(solution)/shard_map/ppermute | solution.py:164
  42.3 6.5 %copy-start.8 = (bf16[8,1152]{1,0:T(8,128)(2,1)}, bf16[8,1152]{1,0:T(8,128)(2,1)S(1)}, u32[]{:S(2)}) copy-start(bf16[8,1152]{1,0:T(8,128)(2,1)S(1)} %collective-permute-done.7.refs_8_) | copy-start | bytes 55300
  42.3 5.0 %collective-permute-start.12 = (bf16[8,1152]{1,0:T(8,128)(2,1)S(1)}, bf16[8,1152]{1,0:T(8,128)(2,1)S(1)}, u32[]{:S(2)}, u32[]{:S(2)}) collective-permute-start(bf16[8,1152]{1,0:T(8,128)(2,1)S(1)} %get-tuple-element.34), channel_id=1, source_target_pairs={{0,13},{1,14},{2,15},{3,0},{4,1},{5,2},{6,3},{7,4},{8,5},{9,6},{10... | collective-permute-start | bytes 55304 | tf_op jit(solution)/shard_map/ppermute | solution.py:164
  43.5 5.3 %copy-start.9 = (bf16[8,1152]{1,0:T(8,128)(2,1)}, bf16[8,1152]{1,0:T(8,128)(2,1)S(1)}, u32[]{:S(2)}) copy-start(bf16[8,1152]{1,0:T(8,128)(2,1)S(1)} %collective-permute-done.8.refs_9_) | copy-start | bytes 55300
  43.5 3.9 %collective-permute-start.13 = (bf16[8,1152]{1,0:T(8,128)(2,1)S(1)}, bf16[8,1152]{1,0:T(8,128)(2,1)S(1)}, u32[]{:S(2)}, u32[]{:S(2)}) collective-permute-start(bf16[8,1152]{1,0:T(8,128)(2,1)S(1)} %get-tuple-element.35), channel_id=1, source_target_pairs={{0,14},{1,15},{2,0},{3,1},{4,2},{5,3},{6,4},{7,5},{8,6},{9,7},{10,... | collective-permute-start | bytes 55304 | tf_op jit(solution)/shard_map/ppermute | solution.py:164
  44.7 4.1 %copy-start.10 = (bf16[8,1152]{1,0:T(8,128)(2,1)}, bf16[8,1152]{1,0:T(8,128)(2,1)S(1)}, u32[]{:S(2)}) copy-start(bf16[8,1152]{1,0:T(8,128)(2,1)S(1)} %collective-permute-done.9.refs_10_) | copy-start | bytes 55300
  44.7 4.0 %collective-permute-start.14 = (bf16[8,1152]{1,0:T(8,128)(2,1)S(1)}, bf16[8,1152]{1,0:T(8,128)(2,1)S(1)}, u32[]{:S(2)}, u32[]{:S(2)}) collective-permute-start(bf16[8,1152]{1,0:T(8,128)(2,1)S(1)} %get-tuple-element.36), channel_id=1, source_target_pairs={{0,15},{1,0},{2,1},{3,2},{4,3},{5,4},{6,5},{7,6},{8,7},{9,8},{10,9... | collective-permute-start | bytes 55304 | tf_op jit(solution)/shard_map/ppermute | solution.py:164
  47.3 1.5 %copy-start.11 = (bf16[8,1152]{1,0:T(8,128)(2,1)}, bf16[8,1152]{1,0:T(8,128)(2,1)S(1)}, u32[]{:S(2)}) copy-start(bf16[8,1152]{1,0:T(8,128)(2,1)S(1)} %collective-permute-done.10.refs_11_) | copy-start | bytes 55300
  47.3 1.5 %copy-start.12 = (bf16[8,1152]{1,0:T(8,128)(2,1)}, bf16[8,1152]{1,0:T(8,128)(2,1)S(1)}, u32[]{:S(2)}) copy-start(bf16[8,1152]{1,0:T(8,128)(2,1)S(1)} %collective-permute-done.11.refs_12_) | copy-start | bytes 55300
  47.3 1.5 %copy-start.13 = (bf16[8,1152]{1,0:T(8,128)(2,1)}, bf16[8,1152]{1,0:T(8,128)(2,1)S(1)}, u32[]{:S(2)}) copy-start(bf16[8,1152]{1,0:T(8,128)(2,1)S(1)} %collective-permute-done.12.refs_13_) | copy-start | bytes 55300
  47.3 1.5 %copy-start.14 = (bf16[8,1152]{1,0:T(8,128)(2,1)}, bf16[8,1152]{1,0:T(8,128)(2,1)S(1)}, u32[]{:S(2)}) copy-start(bf16[8,1152]{1,0:T(8,128)(2,1)S(1)} %collective-permute-done.13.refs_14_) | copy-start | bytes 55300
  48.8 0.6 %copy-start.15 = (bf16[8,1152]{1,0:T(8,128)(2,1)}, bf16[8,1152]{1,0:T(8,128)(2,1)S(1)}, u32[]{:S(2)}) copy-start(bf16[8,1152]{1,0:T(8,128)(2,1)S(1)} %collective-permute-done.14.refs_15_) | copy-start | bytes 55300
